TPU v7x, 256 devices: a whole 4x4x8 slice. The times are simulated.
256 devices in a mesh: lat: 16 (over z, y_hi), lon: 16 (over y_lo, x, core).
Axes of the slice: x: 4, y: 4 (y_hi: 2, y_lo: 2; y = y_hi * 2 + y_lo), z: 8, core: 2. Of those that a mesh axis runs over, the one named last changes fastest.
Arguments:
- fields: bfloat16 [2, 4, 192, 192, 512], P(None, None, 'lat', 'lon'), may hold values from -6 to 6
- valid_rows: int32 [192], P('lat'), may hold values from 0 to 1, as said below
- fine_qkv: bfloat16 [512, 1536], replicated, may hold values from -1 to 1
- fine_out: bfloat16 [512, 512], replicated, may hold values from -0.25 to 0.25
- merge_weight: bfloat16 [2048, 1024], replicated, may hold values from -0.125 to 0.125
- coarse_qkv: bfloat16 [3, 1024, 1024], P(None, 'lat', 'lon'), may hold values from -1 to 1
- coarse_out: bfloat16 [1024, 1024], P('lat', 'lon'), may hold values from -0.1875 to 0.1875
- expand_weight: bfloat16 [1024, 2048], replicated, may hold values from -0.1875 to 0.1875
Outputs:
- decoded: bfloat16 [2, 4, 192, 192, 512], P(None, None, 'lat', 'lon')
Inputs may be any that keep to these rules, and one draw needn't show every extreme that they name: `valid_rows`: the rows with value 1 are the first ones; between 1 and 18 rows at the end are 0.
All inputs are finite; a program needn't handle non-finite values.
Results may differ from a plain program's by a relative error of at most 0.01.
Values may be sent and summed in bfloat16 or wider, within the bound.
A program may use at most 128 MiB of HBM per device.

v0:
```python
import jax
import jax.numpy as jnp
from jax import lax
from jax.sharding import PartitionSpec as P

HEAD_DIM = 32
WIN_LEV = 2
WIN_LAT = 6
WIN_LON = 12


EPSILON = 1e-05


def passed_along(value, axis, steps):
    count = lax.axis_size(axis)
    pairs = [(source, (source + steps) % count) for source in range(count)]
    return lax.ppermute(value, axis, pairs)


def swapped(value, axis, stride):
    mask = 2**stride
    pairs = [(source, source ^ mask) for source in range(lax.axis_size(axis))]
    return lax.ppermute(value, axis, pairs)


def layer_norm(values):
    values = values.astype(jnp.float32)
    centre = values - jnp.mean(values, axis=-1, keepdims=True)
    spread = jnp.mean(centre * centre, axis=-1, keepdims=True)
    return centre * lax.rsqrt(spread + EPSILON)


def attend(queries, keys_all, values, allowed, scale):
    scores = (
        jnp.einsum("bqhd,bkhd->bhqk", queries, keys_all, preferred_element_type=jnp.float32) * scale
    )
    scores = jnp.where(allowed[:, None], scores, -jnp.inf)
    highest = jnp.max(scores, axis=-1, keepdims=True)
    expo = jnp.exp(scores - highest)
    weights = (expo / jnp.sum(expo, axis=-1, keepdims=True)).astype(jnp.bfloat16)
    mixed = jnp.einsum(
        "bhqk,bkhd->bqhd", weights, values, preferred_element_type=jnp.float32
    ).astype(jnp.bfloat16)
    return mixed.reshape(mixed.shape[0], mixed.shape[1], -1)


def shards(
    fields, valid_rows, fine_qkv, fine_out, merge_weight, coarse_qkv, coarse_out, expand_weight
):
    samples, levels, lat_rows, lon_cols, width = fields.shape
    half_lev = WIN_LEV // 2
    half_lat = WIN_LAT // 2
    half_lon = WIN_LON // 2
    lev_groups = levels // WIN_LEV
    lat_groups = lat_rows // WIN_LAT
    window_size = WIN_LEV * WIN_LAT * lon_cols
    scale = HEAD_DIM ** (-0.5)
    band = lax.axis_index("lat")
    tile = lax.axis_index("lon")
    total_rows = lat_rows * lax.axis_size("lat")
    upper, upper_flags = passed_along(
        (fields[:, :, :half_lat], valid_rows[:half_lat].astype(jnp.bfloat16)), "lat", -1
    )
    shifted = jnp.concatenate([fields[:, :, half_lat:], upper], axis=2)
    eastern = passed_along(shifted[:, :, :, :half_lon], "lon", -1)
    shifted = jnp.concatenate([shifted[:, :, :, half_lon:], eastern], axis=3)
    shifted = jnp.roll(shifted, -half_lev, axis=1)
    windows = shifted.reshape(samples, lev_groups, WIN_LEV, lat_groups, WIN_LAT, lon_cols, width)
    windows = windows.transpose(0, 1, 3, 2, 4, 5, 6).reshape(-1, window_size, width)
    level_ids = ((jnp.arange(levels) + half_lev) % levels + half_lev) // WIN_LEV
    row_global = (band * lat_rows + jnp.arange(lat_rows) + half_lat) % total_rows
    row_ids = (row_global + half_lat) // WIN_LAT
    arrived = jnp.where(upper_flags == 1, 1, 0).astype(jnp.int32)
    row_valid = jnp.concatenate([valid_rows[half_lat:], arrived], axis=0)
    grid = (lev_groups, lat_groups, WIN_LEV, WIN_LAT, lon_cols)
    token_level = jnp.broadcast_to(level_ids.reshape(lev_groups, 1, WIN_LEV, 1, 1), grid).reshape(
        -1, window_size
    )
    token_row = jnp.broadcast_to(row_ids.reshape(1, lat_groups, 1, WIN_LAT, 1), grid).reshape(
        -1, window_size
    )
    token_valid = jnp.broadcast_to(row_valid.reshape(1, lat_groups, 1, WIN_LAT, 1), grid).reshape(
        -1, window_size
    )
    allowed = (token_level[:, :, None] == token_level[:, None, :]) & (
        token_row[:, :, None] == token_row[:, None, :]
    )
    allowed = allowed & ((token_valid[:, None, :] == 1) | (token_valid[:, :, None] == 0))
    allowed = jnp.broadcast_to(allowed[None], (samples,) + allowed.shape).reshape(
        -1, window_size, window_size
    )
    keep = jnp.broadcast_to(token_valid[None], (samples,) + token_valid.shape).reshape(
        -1, window_size
    )
    heads = width // HEAD_DIM
    normed = layer_norm(windows).astype(jnp.bfloat16)
    projected = jnp.dot(normed.reshape(-1, width), fine_qkv, preferred_element_type=jnp.float32)
    projected = projected.astype(jnp.bfloat16).reshape(-1, window_size, 3, heads, HEAD_DIM)
    mixed = attend(projected[:, :, 0], projected[:, :, 1], projected[:, :, 2], allowed, scale)
    update = jnp.dot(
        mixed.reshape(-1, width), fine_out, preferred_element_type=jnp.float32
    ).reshape(windows.shape)
    skip_windows = (
        (windows.astype(jnp.float32) + update) * keep.astype(jnp.float32)[:, :, None]
    ).astype(jnp.bfloat16)
    rolled = skip_windows.reshape(
        samples, lev_groups, lat_groups, WIN_LEV, WIN_LAT, lon_cols, width
    )
    rolled = rolled.transpose(0, 1, 3, 2, 4, 5, 6).reshape(fields.shape)
    rolled = jnp.roll(rolled, half_lev, axis=1)
    returned = passed_along(rolled[:, :, :, lon_cols - half_lon :], "lon", 1)
    rolled = jnp.concatenate([returned, rolled[:, :, :, : lon_cols - half_lon]], axis=3)
    returned = passed_along(rolled[:, :, lat_rows - half_lat :], "lat", 1)
    skip = jnp.concatenate([returned, rolled[:, :, : lat_rows - half_lat]], axis=2)
    coarse_rows = lat_rows // 2
    coarse_cols = lon_cols // 2
    parts = skip.reshape(samples, levels, coarse_rows, 2, coarse_cols, 2, width).transpose(
        0, 1, 2, 4, 5, 3, 6
    )
    parts = parts.reshape(-1, 4 * width)
    merged = jnp.dot(
        layer_norm(parts).astype(jnp.bfloat16), merge_weight, preferred_element_type=jnp.float32
    ).astype(jnp.bfloat16)
    wide = merged.shape[-1]
    normed_two = layer_norm(merged).astype(jnp.bfloat16)
    is_west = tile % 2 == 0
    heads_two = wide // HEAD_DIM
    query_count = WIN_LEV * coarse_rows * coarse_cols
    key_count = 2 * query_count
    coarse_valid = valid_rows[0::2]
    query_valid = jnp.broadcast_to(
        coarse_valid[None, :, None], (WIN_LEV, coarse_rows, coarse_cols)
    ).reshape(-1)
    key_valid = jnp.broadcast_to(
        coarse_valid[None, :, None], (WIN_LEV, coarse_rows, 2 * coarse_cols)
    ).reshape(-1)
    qkv_part, out_part = (
        lax.all_gather(coarse_qkv, "lat", axis=1, tiled=True),
        lax.all_gather(coarse_out, "lat", axis=0, tiled=True),
    )
    coarse_proj = jnp.einsum(
        "td,xdc->txc",
        normed_two,
        lax.all_gather(qkv_part, "lon", axis=2, tiled=True),
        preferred_element_type=jnp.float32,
    )
    coarse_proj = coarse_proj.astype(jnp.bfloat16).reshape(
        samples, levels, coarse_rows, coarse_cols, 3, wide
    )
    queries_two = coarse_proj[:, :, :, :, 0]
    paired = coarse_proj[:, :, :, :, 1:]
    partner = swapped(paired, "lon", 0)
    western = jnp.where(is_west, paired, partner)
    easterly = jnp.where(is_west, partner, paired)
    joined = jnp.concatenate([western, easterly], axis=3)
    query_win = queries_two.reshape(samples * lev_groups, query_count, heads_two, HEAD_DIM)
    key_win = joined[:, :, :, :, 0].reshape(samples * lev_groups, key_count, heads_two, HEAD_DIM)
    value_win = joined[:, :, :, :, 1].reshape(samples * lev_groups, key_count, heads_two, HEAD_DIM)
    allowed_two = (key_valid[None, :] == 1) | (query_valid[:, None] == 0)
    allowed_two = jnp.broadcast_to(
        allowed_two[None], (samples * lev_groups, query_count, key_count)
    )
    mixed_two = attend(query_win, key_win, value_win, allowed_two, scale).reshape(-1, wide)
    update_two = jnp.dot(
        mixed_two,
        lax.all_gather(out_part, "lon", axis=1, tiled=True),
        preferred_element_type=jnp.float32,
    )
    coarse = (merged.astype(jnp.float32) + update_two).astype(jnp.bfloat16)
    grown = jnp.dot(coarse, expand_weight, preferred_element_type=jnp.float32)
    grown = grown.reshape(samples, levels, coarse_rows, coarse_cols, 2, 2, width).transpose(
        0, 1, 2, 5, 3, 4, 6
    )
    grown = grown.reshape(samples, levels, lat_rows, lon_cols, width)
    row_keep = valid_rows.astype(jnp.float32)[None, None, :, None, None]
    return ((skip.astype(jnp.float32) + grown) * row_keep).astype(jnp.bfloat16)


def solution(mesh):
    return jax.shard_map(
        shards,
        mesh=mesh,
        in_specs=(
            P(None, None, "lat", "lon", None),
            P("lat"),
            P(),
            P(),
            P(),
            P(None, "lat", "lon"),
            P("lat", "lon"),
            P(),
        ),
        out_specs=P(None, None, "lat", "lon", None),
        check_vma=False,
    )
```

profile of v0, /device:TPU:2, one launch (start us, length us, event | category | flops | bytes accessed | tf_op | source)
XLA Modules:
  0.0 318.0 jit_solution(14606223144348953237)
XLA Ops:
  6.5 1.9 slice.72
  8.4 8.5 %collective-permute-start = (bf16[2,4,3,12,512]{4,1,3,2,0:T(4,128)(2,1)}, bf16[2,4,3,12,512]{4,1,3,2,0:T(4,128)(2,1)}, u32[]{:S(2)}, u32[]{:S(2)}) collective-permute-start(bf16[2,4,3,12,512]{4,1,3,2,0:T(4,128)(2,1)} %slice.72), channel_id=1, source_target_pairs={{0,240},{16,0},{32,16},{48,32},{64,48},{80,64},{96,80},{112,96},{1... | collective-permute-start | bytes 884744 | tf_op jit(solution)/shard_map/ppermute | solution.py:18
  16.9 0.8 copy.90
  17.8 51.7 %all_gather.12 = bf16[3,1024,64]{2,0,1:T(4,128)(2,1)S(1)} all-gather(bf16[3,64,64]{2,0,1:T(4,128)(2,1)S(1)} %copy.90), channel_id=1, replica_groups=mesh['lat'=16,'lon'=16] {'lat'}, dimensions={1}, use_global_device_ids=true | all-gather | bytes 417792 | tf_op jit(solution)/shard_map/all_gather | solution.py:139
  69.5 1.2 copy.91
  71.4 2.6 fusion.42
  74.0 2.0 collective-permute-done.2
  76.9 1.0 or_and_fusion
  77.8 8.1 %collective-permute-done.1 = bf16[2,4,12,6,512]{4,1,3,2,0:T(4,128)(2,1)S(1)} collective-permute-done((bf16[2,4,12,6,512]{4,1,3,2,0:T(4,128)(2,1)}, bf16[2,4,12,6,512]{4,1,3,2,0:T(4,128)(2,1)S(1)}, u32[]{:S(2)}, u32[]{:S(2)}) %collective-permute-start.1) | collective-permute-done | bytes 589856 | tf_op jit(solution)/shard_map/ppermute | solution.py:18
  86.0 1.1 slice_maximum_fusion
  87.0 2.5 fusion.35
  89.5 4.4 %reshape.260 = f32[2,2,2,2,6,12,512]{6,2,1,5,4,3,0:T(2,128)} reshape(f32[2,4,12,12,512]{4,1,3,2,0:T(4,128)} %fusion.35) | data formatting | bytes 4718592 | tf_op jit(solution)/shard_map/convert_element_type | solution.py:105
  93.9 4.1 %copy.154 = f32[2,2,2,2,6,12,512]{6,5,4,2,3,1,0:T(8,128)} copy(f32[2,2,2,2,6,12,512]{6,2,1,5,4,3,0:T(2,128)} %reshape.260) | data formatting | bytes 4718592 | tf_op jit(solution)/shard_map/convert_element_type | solution.py:105
  98.0 4.0 %reshape.265 = f32[8,144,512]{2,1,0:T(8,128)} reshape(f32[2,2,2,2,6,12,512]{6,5,4,3,2,1,0:T(8,128)} %bitcast.85) | data formatting | bytes 4718592 | tf_op jit(solution)/shard_map/convert_element_type | solution.py:105
  102.0 4.0 %reshape.256 = f32[1152,512]{1,0:T(8,128)} reshape(f32[2,2,2,2,6,12,512]{6,5,4,3,2,1,0:T(8,128)} %bitcast.86) | data formatting | bytes 4718592 | tf_op jit(solution)/shard_map/convert_element_type | solution.py:105
  105.9 2.5 fusion.48
  108.5 2.8 multiply_reduce_fusion
  111.5 5.5 %convolution_convert_fusion = bf16[1152,1536]{1,0:T(8,128)(2,1)} fusion(bf16[512,1536]{1,0:T(8,128)(2,1)S(1)} %copy-done, f32[1152,512]{1,0:T(8,128)} %reshape.256, f32[1152]{0:T(1024)S(1)} %rsqrt.31, f32[1152]{0:T(1024)S(1)} %div.59), kind=kOutput, calls=%fused_computation.13 | convolution fusion | flops 1815478272 | bytes 7480320 | tf_op jit(solution)/shard_map/dot_general | solution.py:98
  116.9 4.4 %copy.80 = bf16[1152,1536]{0,1:T(8,128)(2,1)S(1)} copy(bf16[1152,1536]{1,0:T(8,128)(2,1)} %convolution_convert_fusion) | data formatting | bytes 7077888 | tf_op jit(solution)/shard_map/convert_element_type | solution.py:99
  121.3 9.1 %reshape.249 = bf16[8,144,3,16,32]{1,0,4,3,2:T(8,128)(2,1)} reshape(bf16[1152,1536]{0,1:T(8,128)(2,1)S(1)} %copy.80) | data formatting | bytes 7077888 | tf_op jit(solution)/shard_map/reshape | solution.py:99
  130.4 5.6 %fusion.58 = (bf16[8,144,1,16,32]{1,0,4,3,2:T(8,128)(2,1)S(1)}, bf16[8,144,1,16,32]{1,0,4,3,2:T(8,128)(2,1)}, bf16[8,144,1,16,32]{1,0,4,3,2:T(8,128)(2,1)}) fusion(bf16[8,144,3,16,32]{1,0,4,3,2:T(8,128)(2,1)} %reshape.249), kind=kLoop, calls=%fused_computation.113 | loop fusion | bytes 7077888 | tf_op jit(solution)/shard_map/slice | solution.py:100
  136.1 13.0 %fusion.60 = (f32[8,16,144]{2,1,0:T(8,128)S(1)}, f32[8,16,144,144]{2,3,1,0:T(8,128)}) fusion(pred[8,144,144]{1,2,0:T(8,128)(4,1)S(1)} %bitcast.96, bf16[8,144,1,16,32]{1,0,4,3,2:T(8,128)(2,1)} %get-tuple-element.8, bf16[8,144,1,16,32]{1,0,4,3,2:T(8,128)(2,1)} %get-tuple-element.9), kind=kOutput, calls=%fused_computation.115 | convolution fusion | flops 180486288 | bytes 13215744 | tf_op jit(solution)/shard_map/sub | solution.py:40
  149.1 8.1 %fusion.18 = bf16[8,16,32,144]{3,2,1,0:T(8,128)(2,1)S(1)} fusion(f32[8,16,144,144]{2,3,1,0:T(8,128)} %get-tuple-element.23, f32[8,16,144]{2,1,0:T(8,128)S(1)} %get-tuple-element.22, bf16[8,144,1,16,32]{1,0,4,3,2:T(8,128)(2,1)S(1)} %get-tuple-element.7), kind=kOutput, calls=%fused_computation.37 | convolution fusion | flops 175767552 | bytes 13049856 | tf_op jit(solution)/shard_map/bhqk,bkhd->bqhd/dot_general | solution.py:42
  157.2 0.9 multiply_convert_fusion.2
  158.2 0.7 copy.87
  158.8 0.5 reshape.250
  159.3 1.0 copy.88
  160.3 0.2 slice.100
  160.5 0.6 slice.101
  161.2 0.8 fusion.41
  161.9 2.2 collective-permute-start.3
  164.1 7.7 %collective-permute-done.3 = bf16[2,4,12,6,512]{4,0,3,2,1:T(2,128)(2,1)S(1)} collective-permute-done((bf16[2,4,12,6,512]{4,0,3,2,1:T(2,128)(2,1)S(1)}, bf16[2,4,12,6,512]{4,0,3,2,1:T(2,128)(2,1)S(1)}, u32[]{:S(2)}, u32[]{:S(2)}) %collective-permute-start.3) | collective-permute-done | bytes 589856 | tf_op jit(solution)/shard_map/ppermute | solution.py:18
  171.8 0.4 pad_maximum_fusion.5
  172.2 4.6 %collective-permute-start.4 = (bf16[2,4,3,12,512]{4,0,3,2,1:T(2,128)(2,1)S(1)}, bf16[2,4,3,12,512]{4,0,3,2,1:T(2,128)(2,1)S(1)}, u32[]{:S(2)}, u32[]{:S(2)}) collective-permute-start(bf16[2,4,3,12,512]{4,0,3,2,1:T(2,128)(2,1)S(1)} %pad_maximum_fusion.5), channel_id=1, source_target_pairs={{0,16},{16,32},{32,48},{48,64},{64,80},{80,96},{96,112},{112,128},... | collective-permute-start | bytes 884744 | tf_op jit(solution)/shard_map/ppermute | solution.py:18
  176.7 7.2 %collective-permute-done.4 = bf16[2,4,3,12,512]{4,0,3,2,1:T(2,128)(2,1)S(1)} collective-permute-done((bf16[2,4,3,12,512]{4,0,3,2,1:T(2,128)(2,1)S(1)}, bf16[2,4,3,12,512]{4,0,3,2,1:T(2,128)(2,1)S(1)}, u32[]{:S(2)}, u32[]{:S(2)}) %collective-permute-start.4) | collective-permute-done | bytes 294944 | tf_op jit(solution)/shard_map/ppermute | solution.py:18
  183.9 1.6 fusion.33
  185.6 3.2 %copy.155 = f32[2,4,6,2,6,2,512]{6,3,5,4,2,1,0:T(2,128)} copy(f32[2,4,6,2,6,2,512]{6,0,5,4,3,2,1:T(2,128)S(1)} %bitcast.82) | data formatting | bytes 4718592 | tf_op jit(solution)/shard_map/convert_element_type | solution.py:28
  188.8 4.2 %reshape.257 = f32[288,2048]{1,0:T(8,128)} reshape(f32[2,4,6,6,2,2,512]{6,5,4,3,2,1,0:T(2,128)} %bitcast.89) | data formatting | bytes 4718592 | tf_op jit(solution)/shard_map/convert_element_type | solution.py:28
  193.0 2.2 fusion.56
  195.2 0.1 div.68
  195.3 2.5 multiply_reduce_fusion.1
  197.9 4.5 %convert_reduce_fusion = (f32[288]{0:T(512)S(1)}, bf16[288,1024]{1,0:T(8,128)(2,1)S(1)}) fusion(bf16[2048,1024]{1,0:T(8,128)(2,1)} %param.12, f32[288,2048]{1,0:T(8,128)} %reshape.257, f32[288]{0:T(512)S(1)} %rsqrt.33, f32[288]{0:T(512)S(1)} %div.68), kind=kOutput, calls=%fused_computation.41 | convolution fusion | flops 1210613504 | bytes 7146880 | tf_op jit(solution)/shard_map/dot_general | solution.py:122
  202.4 0.3 fusion.30
  202.8 0.5 copy-done.7
  203.3 6.1 %convolution_convert_fusion.1 = bf16[288,3,1024]{2,0,1:T(8,128)(2,1)} fusion(bf16[3,1024,1024]{1,2,0:T(8,128)(2,1)} %all-gather.3.cloned.1.call-done, bf16[288,1024]{1,0:T(8,128)(2,1)S(1)} %get-tuple-element.25, f32[288]{0:T(512)S(1)} %add_rsqrt_fusion.2, f32[288]{0:T(512)S(1)} %broadcast_multiply_fusion.2), kind=kOutput, calls=%fused_computation.42 | convolution fusion | flops 1814003712 | bytes 8653056 | tf_op jit(solution)/shard_map/td,xdc->txc/dot_general | solution.py:142
  209.4 2.5 reshape.252
  212.1 1.9 copy.92
  214.0 39.3 %all_gather.14 = bf16[1024,64]{1,0:T(8,128)(2,1)S(1)} all-gather(bf16[64,64]{1,0:T(8,128)(2,1)S(1)} %copy-done.10), channel_id=1, replica_groups=mesh['lat'=16,'lon'=16] {'lat'}, dimensions={0}, use_global_device_ids=true | all-gather | bytes 139264 | tf_op jit(solution)/shard_map/all_gather | solution.py:140
  253.3 0.8 copy.99
  254.7 3.1 reshape_squeeze.10
  257.8 2.7 copy_select_fusion.1
  260.5 2.5 fusion.20
  263.1 4.9 %reshape_squeeze.11 = bf16[4,144,32,32]{3,2,1,0:T(8,128)(2,1)} reshape(bf16[2,4,6,12,1,1024]{5,3,2,1,0,4:T(8,128)(2,1)S(1)} %get-tuple-element.13) | data formatting | bytes 2359296 | tf_op jit(solution)/shard_map/reshape;squeeze | solution.py:158
  268.0 6.8 %reshape_squeeze.9 = bf16[4,144,32,32]{3,2,1,0:T(8,128)(2,1)} reshape(bf16[2,4,6,12,1,1024]{5,3,2,1,0,4:T(8,128)(2,1)} %get-tuple-element.12) | data formatting | bytes 2359296 | tf_op jit(solution)/shard_map/reshape;squeeze | solution.py:159
  274.8 5.7 %fusion.12 = f32[4,32,72,144]{3,2,1,0:T(8,128)S(1)} fusion(bf16[4,144,32,32]{3,2,1,0:T(8,128)(2,1)} %reshape_squeeze.11, bf16[4,72,32,32]{3,2,1,0:T(8,128)(2,1)S(1)} %copy-done.5), kind=kOutput, calls=%fused_computation.18 | convolution fusion | flops 84934656 | bytes 7077888 | tf_op jit(solution)/shard_map/bqhd,bkhd->bhqk/dot_general | solution.py:36
  280.5 7.3 %fusion.61 = (f32[4,32,72]{2,1,0:T(8,128)S(1)}, f32[4,32,72,144]{3,2,1,0:T(8,128)}) fusion(f32[4,32,72,144]{3,2,1,0:T(8,128)S(1)} %fusion.12, pred[72,144]{1,0:T(8,128)(4,1)S(1)} %broadcast_or_fusion), kind=kOutput, calls=%fused_computation.116 | output fusion | flops 7962767 | bytes 10664064 | tf_op jit(solution)/shard_map/sub | solution.py:40
  287.8 5.8 %fusion.26 = bf16[4,72,32,32]{1,3,2,0:T(8,128)(2,1)S(1)} fusion(f32[4,32,72,144]{3,2,1,0:T(8,128)} %get-tuple-element.27, f32[4,32,72]{2,1,0:T(8,128)S(1)} %get-tuple-element.26, bf16[4,144,32,32]{3,2,1,0:T(8,128)(2,1)S(1)} %bitcast.91), kind=kOutput, calls=%fused_computation.50 | convolution fusion | flops 87883776 | bytes 7114752 | tf_op jit(solution)/shard_map/bhqk,bkhd->bqhd/dot_general | solution.py:42
  293.6 0.8 copy.98
  294.4 0.7 reshape_reshape.4
  295.1 6.6 %fusion.40 = f32[288,2048]{1,0:T(8,128)} fusion(bf16[1024,2048]{1,0:T(8,128)(2,1)} %param.15, bf16[288,1024]{0,1:T(8,128)(2,1)S(1)} %reshape_reshape.4, bf16[1024,1024]{0,1:T(8,128)(2,1)} %all-gather.5.cloned.1.call-done, bf16[288,1024]{1,0:T(8,128)(2,1)S(1)} %copy-done.8), kind=kOutput, calls=%fused_computation.71 | convolution fusion | flops 1812824064 | bytes 9830400 | tf_op jit(solution)/shard_map/dot_general | solution.py:171
  301.8 3.3 %reshape.253 = f32[2,4,6,6,2,2,512]{6,5,4,3,2,1,0:T(2,128)S(1)} reshape(f32[288,2048]{1,0:T(8,128)} %fusion.40) | data formatting | bytes 4718592 | tf_op jit(solution)/shard_map/reshape | solution.py:172
  305.1 1.8 copy.100
  307.0 1.8 multiply_convert_fusion
  308.8 1.9 copy.101
  (82 shorter events, 2.7 us)
Async XLA Ops:
  6.5 104.9 %copy-start = (bf16[512,1536]{1,0:T(8,128)(2,1)S(1)}, bf16[512,1536]{1,0:T(8,128)(2,1)}, u32[]{:S(2)}) copy-start(bf16[512,1536]{1,0:T(8,128)(2,1)} %param.10) | copy-start | bytes 4718596
  6.5 64.3 %copy-start.11 = (s32[12]{0:T(128)S(1)}, s32[12]{0:T(128)}, u32[]{:S(2)}) copy-start(s32[12]{0:T(128)} %param.9) | copy-start | bytes 148
  6.5 196.2 %all-gather.3.cloned.1.call-start = ((), (), s32[]{:S(2)}) async-start(), calls=%async_computation | async-start | bytes 6684672 | tf_op jit(solution)/shard_map/all_gather | solution.py:145
  8.4 62.9 %collective-permute-start = (bf16[2,4,3,12,512]{4,1,3,2,0:T(4,128)(2,1)}, bf16[2,4,3,12,512]{4,1,3,2,0:T(4,128)(2,1)}, u32[]{:S(2)}, u32[]{:S(2)}) collective-permute-start(bf16[2,4,3,12,512]{4,1,3,2,0:T(4,128)(2,1)} %slice.72), channel_id=1, source_target_pairs={{0,240},{16,0},{32,16},{48,32},{64,48},{80,64},{96,80},{112,96},{1... | collective-permute-start | bytes 884744 | tf_op jit(solution)/shard_map/ppermute | solution.py:18
  17.8 53.6 %slice-start.2 = ((bf16[2,4,12,12,512]{4,1,3,2,0:T(4,128)(2,1)}), bf16[2,4,9,12,512]{4,1,3,2,0:T(4,128)(2,1)S(1)}, s32[]{:S(2)}) async-start(bf16[2,4,12,12,512]{4,1,3,2,0:T(4,128)(2,1)} %param.8), calls=%async_computation.4 | async-start | bytes 1769472 | tf_op jit(solution)/shard_map/slice | solution.py:65
  70.8 224.3 %all-gather.5.cloned.1.call-start = ((), (), s32[]{:S(2)}) async-start(), calls=%async_computation.1 | async-start | bytes 2228224 | tf_op jit(solution)/shard_map/all_gather | solution.py:167
  70.8 5.1 %collective-permute-start.2 = (bf16[3]{0:T(256)(128)(2,1)S(1)}, bf16[3]{0:T(256)(128)(2,1)S(1)}, u32[]{:S(2)}, u32[]{:S(2)}) collective-permute-start(bf16[3]{0:T(256)(128)(2,1)S(1)} %bitcast.97), channel_id=1, source_target_pairs={{0,240},{16,0},{32,16},{48,32},{64,48},{80,64},{96,80},{112,96},{1... | collective-permute-start | bytes 26 | tf_op jit(solution)/shard_map/ppermute | solution.py:18
  74.0 12.0 %collective-permute-start.1 = (bf16[2,4,12,6,512]{4,1,3,2,0:T(4,128)(2,1)}, bf16[2,4,12,6,512]{4,1,3,2,0:T(4,128)(2,1)S(1)}, u32[]{:S(2)}, u32[]{:S(2)}) collective-permute-start(bf16[2,4,12,6,512]{4,1,3,2,0:T(4,128)(2,1)} %get-tuple-element.15), channel_id=1, source_target_pairs={{0,15},{1,0},{2,1},{3,2},{4,3},{5,4},{6,5},{7,6},{8,7},{9,8},{10,9... | collective-permute-start | bytes 1769480 | tf_op jit(solution)/shard_map/ppermute | solution.py:18
  130.4 5.6 %copy-start.6 = (pred[4,144,144]{1,2,0:T(8,128)(4,1)S(1)}, pred[4,144,144]{1,2,0:T(8,128)(4,1)}, u32[]{:S(2)}) copy-start(pred[4,144,144]{1,2,0:T(8,128)(4,1)} %or_and_fusion) | copy-start | bytes 248836
  149.1 8.2 %copy-start.4 = (f32[8,144,512]{2,1,0:T(8,128)S(1)}, f32[8,144,512]{2,1,0:T(8,128)}, u32[]{:S(2)}) copy-start(f32[8,144,512]{2,1,0:T(8,128)} %reshape.265) | copy-start | bytes 7077892
  149.1 8.2 %copy-start.9 = (bf16[512,512]{1,0:T(8,128)(2,1)S(1)}, bf16[512,512]{1,0:T(8,128)(2,1)}, u32[]{:S(2)}) copy-start(bf16[512,512]{1,0:T(8,128)(2,1)} %param.11) | copy-start | bytes 1572868
  161.9 9.8 %collective-permute-start.3 = (bf16[2,4,12,6,512]{4,0,3,2,1:T(2,128)(2,1)S(1)}, bf16[2,4,12,6,512]{4,0,3,2,1:T(2,128)(2,1)S(1)}, u32[]{:S(2)}, u32[]{:S(2)}) collective-permute-start(bf16[2,4,12,6,512]{4,0,3,2,1:T(2,128)(2,1)S(1)} %fusion.41), channel_id=1, source_target_pairs={{0,1},{1,2},{2,3},{3,4},{4,5},{5,6},{6,7},{7,8},{8,9},{9,10},{10,1... | collective-permute-start | bytes 1769480 | tf_op jit(solution)/shard_map/ppermute | solution.py:18
  172.2 11.8 %collective-permute-start.4 = (bf16[2,4,3,12,512]{4,0,3,2,1:T(2,128)(2,1)S(1)}, bf16[2,4,3,12,512]{4,0,3,2,1:T(2,128)(2,1)S(1)}, u32[]{:S(2)}, u32[]{:S(2)}) collective-permute-start(bf16[2,4,3,12,512]{4,0,3,2,1:T(2,128)(2,1)S(1)} %pad_maximum_fusion.5), channel_id=1, source_target_pairs={{0,16},{16,32},{32,48},{48,64},{64,80},{80,96},{96,112},{112,128},... | collective-permute-start | bytes 884744 | tf_op jit(solution)/shard_map/ppermute | solution.py:18
  185.6 9.8 %copy-start.2 = (f32[2,4,12,12,512]{4,0,3,2,1:T(2,128)}, f32[2,4,12,12,512]{4,0,3,2,1:T(2,128)S(1)}, u32[]{:S(2)}) copy-start(f32[2,4,12,12,512]{4,0,3,2,1:T(2,128)S(1)} %fusion.33) | copy-start | bytes 7077892
  202.4 0.9 copy-start.7
  211.9 2.1 copy-start.10
  214.0 43.8 %collective-permute-start.5 = (bf16[2,4,6,6,2,1024]{5,1,4,3,2,0:T(4,128)(2,1)}, bf16[2,4,6,6,2,1024]{5,1,4,3,2,0:T(4,128)(2,1)}, u32[]{:S(2)}, u32[]{:S(2)}) collective-permute-start(bf16[2,4,6,6,2,1024]{5,1,4,3,2,0:T(4,128)(2,1)} %copy.92), channel_id=1, source_target_pairs={{0,1},{1,0},{2,3},{3,2},{4,5},{5,4},{6,7},{7,6},{8,9},{9,8},{10,11... | collective-permute-start | bytes 3538952 | tf_op jit(solution)/shard_map/ppermute | solution.py:24
  268.0 6.8 %copy-start.5 = (bf16[4,72,32,32]{3,2,1,0:T(8,128)(2,1)S(1)}, bf16[4,72,32,32]{3,2,1,0:T(8,128)(2,1)}, u32[]{:S(2)}) copy-start(bf16[4,72,32,32]{3,2,1,0:T(8,128)(2,1)} %reshape_squeeze.10) | copy-start | bytes 1769476
  274.8 12.9 %slice-start = ((s8[4718592]{0:T(1024)(128)(4,1)}), s8[524288]{0:T(1024)(128)(4,1)S(1)}, s32[]{:S(2)}) async-start(s8[4718592]{0:T(1024)(128)(4,1)} %bitcast.90), calls=%async_computation.2 | async-start | bytes 1048576
  280.5 7.3 %slice-start.1 = ((s8[4718592]{0:T(1024)(128)(4,1)}), s8[4194304]{0:T(1024)(128)(4,1)S(1)}, s32[]{:S(2)}) async-start(s8[4718592]{0:T(1024)(128)(4,1)} %bitcast.90), calls=%async_computation.3 | async-start | bytes 8388608
  293.6 1.5 copy-start.8
  305.1 1.8 copy-start.3
  306.9 3.8 %copy-start.1 = (bf16[512,1536]{1,0:T(8,128)(2,1)S(1)}, bf16[512,1536]{1,0:T(8,128)(2,1)}, u32[]{:S(2)}) copy-start(bf16[512,1536]{1,0:T(8,128)(2,1)} %param.10) | copy-start | bytes 4718596
Sparse Core Ops, SparseCore 0:
  70.9 43.7 all-gather.2
  254.2 30.1 all-gather.4
where the time goes:
time: 324 us; the launch traced here: 318 us
  blocking collectives  91 us (28%)
  local copies, waits for them, and re-layouts  81.4 us (25%)
  matrix products  56.2 us (17%)
  other arithmetic  34.7 us (11%)
  waiting for transfers between devices  25.1 us (8%)
  starting transfers between devices  15.4 us (5%)
  between operations  14.4 us (4%)
    all_gather x1, blocking collectives, shards(): lax.all_gather(coarse_qkv, 'lat', axis=1, tiled=True)  51.7 us
    all_gather x1, blocking collectives, shards(): lax.all_gather(coarse_out, 'lat', axis=0, tiled=True)  39.3 us
    ppermute x5, waiting for transfers between devices, passed_along(): return lax.ppermute(value, axis, pairs)  25 us
    convert_element_type x4, local copies, waits for them, and re-layouts, shards(): windows.astype(jnp.float32) + update  16.4 us
    ppermute x5, starting transfers between devices, passed_along(): return lax.ppermute(value, axis, pairs)  15.3 us
    dot_general x2, matrix products, attend(): jnp.einsum('bhqk,bkhd->bqhd', weights, values, preferred_element_type=jnp...  13.9 us
    sub x1, matrix products, attend(): expo = jnp.exp(scores - highest)  13 us
    reshape x1, local copies, waits for them, and re-layouts, shards(): projected.astype(jnp.bfloat16).reshape(-1, window_size, 3, heads, HEAD_DIM)  9.09 us
  transfers between devices with their start and end apart: 8, of which 4 were waited for; matrix products, arithmetic and copies ran while one was open for 45% of the time, Pallas kernels for 0%

commit v1 on v0

v1 whole, which is shorter than its diff:
```python
import math

import jax
import jax.numpy as jnp
import numpy as np
from jax import lax
from jax.experimental import pallas as pl
from jax.experimental.pallas import tpu as pltpu
from jax.sharding import PartitionSpec as P

BF = jnp.bfloat16
F32 = jnp.float32
MESH = pl.DeviceIdType.MESH
EPSILON = 1e-05
NEG = -1e30
QSCALE = 32 ** (-0.5) * math.log2(math.e)

SEG = (0, 112, 224, 272, 320)
LEVELS = ((1, 2), (3, 0))
PADC = 80


def segment_row(l2, r, c):
    if r >= 3:
        base, rows, row = (0, 9, r - 3) if c >= 6 else (112, 9, r - 3)
    else:
        base, rows, row = (224, 3, r) if c >= 6 else (272, 3, r)
    return base + (l2 * rows + row) * 6 + c % 6


def window_row(l2, r, c):
    window, row = (0, r - 3) if 3 <= r < 9 else (1, r - 9 if r >= 9 else r + 3)
    column = c - 6 if c >= 6 else c + 6
    return window * 144 + l2 * 72 + row * 12 + column


def coarse_row(level, row, column):
    return (level // 2) * PADC + (level % 2) * 36 + row * 6 + column


def tables():
    p1 = np.zeros((2, 320, 192), np.float32)
    p2 = np.zeros((288, 320), np.float32)
    p4 = np.zeros((4 * 2 * PADC, 640), np.float32)
    p5 = np.zeros((768, 4 * 2 * PADC), np.float32)
    for r in range(12):
        for c in range(12):
            plane = (r % 2) + 2 * (c % 2)
            for l2 in range(2):
                seg = segment_row(l2, r, c)
                p1[l2, seg, r * 16 + c] = 1
                p2[window_row(l2, r, c), seg] = 1
                for lg in range(2):
                    level = LEVELS[lg][l2]
                    low = plane * 2 * PADC + coarse_row(level, r // 2, c // 2)
                    p4[low, lg * 320 + seg] = 1
                    p5[level * 192 + r * 16 + c, low] = 1
    rows = np.zeros((2, 144, 32), np.float32)
    differ = np.zeros((144, 144), np.float32)
    level = np.zeros((144, 144), np.float32)
    for t in range(144):
        r6 = (t % 72) // 12
        rows[0, t, 3 + r6] = 1
        rows[1, t, 9 + r6 if r6 < 3 else 16 + r6 - 3] = 1
        for u in range(144):
            differ[t, u] = (r6 < 3) != ((u % 72) // 12 < 3)
            level[t, u] = (t // 72) != (u // 72)
    rows_t = np.zeros((2, 256, 144), np.float32)
    rows_t[:, 0:12] = rows.transpose(0, 2, 1)[:, 0:12]
    rows_t[:, 128:131] = rows.transpose(0, 2, 1)[:, 16:19]
    coarse = np.zeros((PADC, 16), np.float32)
    keep = np.zeros((2, 2 * PADC, 16), np.float32)
    for t in range(72):
        row = (t % 36) // 6
        coarse[t, 2 * row] = 1
        for group in range(2):
            for parity in range(2):
                keep[parity, group * PADC + t, 2 * row + parity] = 1
    coarse_t = np.zeros((128, 2 * PADC), np.float32)
    coarse_t[0:16, :PADC] = coarse.T
    coarse_t[0:16, PADC:] = coarse.T
    pads = np.zeros((8, 2 * PADC), np.float32)
    pads[:, np.arange(2 * PADC) % PADC >= 72] = 1
    half = [jnp.asarray(a, BF) for a in (p1, rows, rows_t, coarse, coarse_t, keep)]
    full = [jnp.asarray(a, F32) for a in (level, differ, pads)]
    late = [jnp.asarray(a, BF) for a in (p2, p2.T.copy(), p4, p5)]
    return half + full, late


def dot(a, b):
    return jnp.dot(a, b, preferred_element_type=F32)


def dot_nt(a, b):
    return lax.dot_general(a, b, (((1,), (1,)), ((), ())), preferred_element_type=F32)


def normalised(x, width):
    mean = jnp.sum(x, axis=-1, keepdims=True) * (1.0 / width)
    centre = x - mean
    spread = jnp.sum(centre * centre, axis=-1, keepdims=True) * (1.0 / width)
    return centre * lax.rsqrt(spread + EPSILON)


def attention(q4, k4, v4, bias):
    count, keys = q4.shape[0], k4.shape[0]
    head = lax.broadcasted_iota(jnp.int32, (16, 128), 1) // 32
    stacked = []
    for h in range(4):
        mask = jnp.where(head == h, 1.0, 0.0).astype(BF)[0:1]
        stacked.append(q4 * mask)
    scores = dot_nt(jnp.concatenate(stacked, axis=0), k4).reshape(4, count, keys) + bias[None]
    highest = jnp.max(scores, axis=-1, keepdims=True)
    expo = jnp.exp2(scores - highest).astype(BF).reshape(4 * count, keys)
    values = jnp.concatenate([v4, jnp.ones((keys, 128), BF)], axis=1)
    mixed = dot(expo, values)
    lanes = lax.broadcasted_iota(jnp.int32, (count, 128), 1) // 32
    top, low = mixed[:count, :128], mixed[:count, 128:]
    for h in range(1, 4):
        part = mixed[h * count : (h + 1) * count]
        top = jnp.where(lanes == h, part[:, :128], top)
        low = jnp.where(lanes == h, part[:, 128:], low)
    return (top / low).astype(BF)


def kernel(
    xp, fl, cw, p1, r1, rt, rc, rct, rk, lm, dm, pads,
    p2_h, p3_h, p4_h, p5_h, wqkv_h, wo_h, wm_h, we_h,
    out,
    p2, p3, p4, p5, wqkv, wo, wm, we,
    snd, xb, ret, zb, fln, pb, wg,
    xw, q, k, v, at, kcol, bias, cbias, krow,
    skp, nbm, mg, n2, q2, kv2, a2, co, dc,
    hs, hr, rs, rr, fs, fr, ps, pr, zs, zr, s2s, s2r, s3s, s3r, ls, lr, ds_, dr, ns, nr, ws,
):
    lat = lax.axis_index("lat")
    lon = lax.axis_index("lon")
    z, y_hi = lat // 2, lat % 2
    y_lo, x, c = lon // 8, (lon // 2) % 4, lon % 2
    y = y_hi * 2 + y_lo

    def device(z_, y_, x_, c_):
        return (z_ * 2 + y_ // 2, (y_ % 2) * 8 + x_ * 2 + c_)

    north, south = (lat + 15) % 16, (lat + 1) % 16
    west, east = (lon + 15) % 16, (lon + 1) % 16
    partner = device(z, y, x, 1 - c)

    barrier = pltpu.get_barrier_semaphore()
    greeted = [partner, (lat, west), (lat, east), (north, lon), (south, lon), (north, west), (south, east)]
    greeted += [device((z + d) % 8, y, x, c) for d in range(1, 8)]
    greeted += [device(z, (y + d) % 4, x, c) for d in range(1, 4)]
    greeted += [device(z, y, (x + d) % 4, c) for d in range(1, 4)]
    for target in greeted:
        pl.semaphore_signal(barrier, inc=1, device_id=target, device_id_type=MESH)

    late = list(zip((p2_h, wqkv_h, wo_h, p3_h, p4_h, wm_h, we_h, p5_h), (p2, wqkv, wo, p3, p4, wm, we, p5)))
    loads = [pltpu.make_async_copy(a, b, ws.at[n]) for n, (a, b) in enumerate(late)]
    for copy in loads:
        copy.start()

    def remote(src, dst, send, recv, target):
        return pltpu.make_async_remote_copy(
            src_ref=src, dst_ref=dst, send_sem=send, recv_sem=recv, device_id=target, device_id_type=MESH
        )

    def halo(i):
        targets = ((lat, west), (north, lon), (north, west))
        return [
            remote(snd.at[i, SEG[n + 1] : SEG[n + 2]], xb.at[i, SEG[n + 1] : SEG[n + 2]], hs.at[i, n], hr.at[i, n], targets[n])
            for n in range(3)
        ]

    def back(i):
        targets = ((lat, east), (south, lon), (south, east))
        return [
            remote(ret.at[i, SEG[n + 1] : SEG[n + 2]], zb.at[i, SEG[n + 1] : SEG[n + 2]], rs.at[i, n], rr.at[i, n], targets[n])
            for n in range(3)
        ]

    flags = remote(fl, fln, fs.at[0], fr.at[0], (north, lon))
    pair = remote(cw, pb, ps.at[0], pr.at[0], partner)

    def along_z():
        block = wg.at[y_lo, x, :, z, y_hi, c]
        return [remote(block, block, zs.at[d - 1], zr.at[d - 1], device((z + d) % 8, y, x, c)) for d in range(1, 8)]

    def second():
        block = wg.at[y_lo, x, :, :, y_hi, c]
        return [
            remote(block, block, s2s.at[d - 1], s2r.at[d - 1], device(z, (y + d * (1 - c)) % 4, (x + d * c) % 4, c))
            for d in range(1, 4)
        ]

    def chunk(core, step, matrices):
        if core == 0:
            return wg.at[:, (x + step) % 4, matrices, :, :, 0]
        other = (y + step) % 4
        return wg.at[other % 2, :, matrices, :, other // 2, 1]

    def ring(core, step):
        return device(z, y, (x + step) % 4, core) if core == 0 else device(z, (y + step) % 4, x, core)

    every = slice(0, 4)

    def third(core):
        block = chunk(core, 0, every)
        return [remote(block, block, s3s.at[n], s3r.at[n], ring(core, step)) for n, step in enumerate((1, 3))]

    def relay(core):
        moves = ((1, 3, slice(0, 2)), (3, 1, slice(2, 4)))
        return [
            remote(chunk(core, s, m), chunk(core, s, m), ls.at[n], lr.at[n], ring(core, to))
            for n, (to, s, m) in enumerate(moves)
        ]

    def across(core, n):
        block = chunk(core, (0, 3, 1, 2)[n], every)
        return remote(block, block, ds_.at[n], dr.at[n], partner)

    def on_core(action):
        @pl.when(c == 0)
        def _():
            action(0)

        @pl.when(c == 1)
        def _():
            action(1)

    pl.semaphore_wait(barrier, len(greeted))
    pair.start()
    flags.start()

    for i in range(4):
        s, (first, last) = i // 2, LEVELS[i % 2]
        tokens = (dot(p1[0], xp[s, first]) + dot(p1[1], xp[s, last])).astype(BF)
        snd[i] = tokens
        xb[i, 0:112] = tokens[0:112]
        for copy in halo(i):
            copy.start()

    pair.wait_recv()
    block = cw[...] + pb[...]
    wg[y_lo, x, :, z, y_hi, c] = jnp.where(c == 0, block[:, :32], block[:, 32:])
    for copy in along_z():
        copy.start()

    flags.wait_recv()
    own, following = fl[...], fln[...]
    seam = jnp.where(lat == 15, NEG, 0.0)
    for w in range(2):
        down = dot(r1[w, :, 0:16], own[0:16]) + dot(r1[w, :, 16:32], following[0:16])
        flat = dot(own[16:32], rt[w, 0:128]) + dot(following[16:32], rt[w, 128:256])
        kcol[w * 144 : (w + 1) * 144] = down
        forbid = ((1.0 - flat[0:1]) * down[:, 0:1]) * NEG
        if w == 1:
            forbid = forbid + dm[...] * seam
        bias[0, w] = forbid
        bias[1, w] = forbid + lm[...] * NEG
    down = dot(rc[...], own[0:16])
    flat = dot(own[16:32], rct[...])
    cbias[...] = ((1.0 - flat[0:1]) * down[:, 0:1] + pads[0:1]) * NEG
    for parity in range(2):
        krow[parity] = dot(rk[parity], own[0:16])

    for copy in loads[0:4]:
        copy.wait()

    def fine(i, carry):
        @pl.when(i == 1)
        def _():
            for copy in along_z():
                copy.wait_recv()
            for copy in second():
                copy.start()

        @pl.when(i == 2)
        def _():
            for copy in second():
                copy.wait_recv()

            def go(core):
                for copy in third(core):
                    copy.start()
                across(core, 0).start()

            on_core(go)

        for copy in halo(i):
            copy.wait_recv()
        tokens = dot(p2[...], xb[i])
        xw[...] = tokens
        normed = normalised(tokens, 512).astype(BF)
        q[...] = (dot(normed, wqkv[:, 0:512]) * QSCALE).astype(BF)
        k[...] = dot(normed, wqkv[:, 512:1024]).astype(BF)
        v[...] = dot(normed, wqkv[:, 1024:1536]).astype(BF)
        group = i % 2

        def heads(g, carry):
            lanes = pl.ds(pl.multiple_of(g * 128, 128), 128)
            for w in range(2):
                rows = slice(w * 144, (w + 1) * 144)
                at[rows, lanes] = attention(q[rows, lanes], k[rows, lanes], v[rows, lanes], bias[group, w])
            return carry

        lax.fori_loop(0, 4, heads, 0)
        skip = ((xw[...] + dot(at[...], wo[...])) * kcol[:, 0:1]).astype(BF)
        tokens = dot(p3[...], skip).astype(BF)
        ret[i] = tokens
        zb[i, 0:112] = tokens[0:112]
        for copy in back(i):
            copy.start()
        return carry

    lax.fori_loop(0, 4, fine, 0)

    def go(core):
        for copy in third(core):
            copy.wait_recv()
        for copy in relay(core):
            copy.start()
        across(core, 1).start()
        across(core, 2).start()

    on_core(go)
    for copy in loads[4:]:
        copy.wait()

    for s in range(2):
        for i in (2 * s, 2 * s + 1):
            for copy in back(i):
                copy.wait_recv()
        planes = dot(p4[...], zb[2 * s : 2 * s + 2].reshape(640, 512))
        skp[s] = planes.astype(BF)
        planes = planes.reshape(4, 160, 512)
        mean = jnp.sum(jnp.sum(planes, axis=0), axis=-1, keepdims=True) * (1.0 / 2048)
        centre = planes - mean[None]
        spread = jnp.sum(jnp.sum(centre * centre, axis=0), axis=-1, keepdims=True) * (1.0 / 2048)
        nbm[:, s * 160 : (s + 1) * 160] = (centre * lax.rsqrt(spread + EPSILON)[None]).astype(BF)

    def merge(n, carry):
        lanes = pl.ds(pl.multiple_of(n * 256, 256), 256)
        total = dot(nbm[0], wm[0:512, lanes])
        for p in range(1, 4):
            total = total + dot(nbm[p], wm[512 * p : 512 * (p + 1), lanes])
        mg[:, lanes] = total.astype(BF)
        return carry

    lax.fori_loop(0, 4, merge, 0)
    n2[0] = normalised(mg[...].astype(F32), 1024).astype(BF)
    swap = remote(n2.at[0], n2.at[1], ns.at[0], nr.at[0], partner)
    swap.start()

    def go(core):
        for copy in relay(core):
            copy.wait_recv()
        across(core, 3).start()

    on_core(go)

    def go(core):
        for n in range(4):
            across(core, n).wait_recv()

    on_core(go)

    def weights(matrix, n):
        low = (n % 2) * 2
        pieces = [wg[n // 2, low + j, matrix].reshape(1024, 128) for j in range(2)]
        return jnp.concatenate(pieces, axis=1)

    def queries(n, carry):
        lanes = pl.ds(pl.multiple_of(n * 256, 256), 256)
        q2[:, lanes] = (dot(n2[0], weights(0, n)) * QSCALE).astype(BF)
        return carry

    lax.fori_loop(0, 4, queries, 0)
    swap.wait_recv()

    def keys(n, carry):
        matrix, block = n // 4, n % 4
        lanes = pl.ds(pl.multiple_of(block * 256, 256), 256)
        kv2[matrix, :, lanes] = dot(n2[...].reshape(640, 1024), weights(matrix + 1, block)).astype(BF)
        return carry

    lax.fori_loop(0, 8, keys, 0)

    def heads(g, carry):
        lanes = pl.ds(pl.multiple_of(g * 128, 128), 128)
        for j in range(4):
            rows, far = slice(j * PADC, (j + 1) * PADC), slice(320 + j * PADC, 320 + (j + 1) * PADC)
            k4 = jnp.concatenate([kv2[0, rows, lanes], kv2[0, far, lanes]], axis=0)
            v4 = jnp.concatenate([kv2[1, rows, lanes], kv2[1, far, lanes]], axis=0)
            a2[rows, lanes] = attention(q2[rows, lanes], k4, v4, cbias[...])
        return carry

    lax.fori_loop(0, 8, heads, 0)

    def project(n, carry):
        lanes = pl.ds(pl.multiple_of(n * 256, 256), 256)
        co[:, lanes] = (mg[:, lanes].astype(F32) + dot(a2[...], weights(3, n))).astype(BF)
        return carry

    lax.fori_loop(0, 4, project, 0)

    def expand(n, carry):
        plane, side = n // 2, n % 2
        grown = dot(co[...], we[:, pl.ds(pl.multiple_of(n * 256, 256), 256)])
        rows = pl.ds(pl.multiple_of(plane * 160, 160), 160)
        lanes = pl.ds(pl.multiple_of(side * 256, 256), 256)
        keep = krow[plane % 2][:, 0:1]
        for s in range(2):
            dc[s, rows, lanes] = ((skp[s, rows, lanes].astype(F32) + grown[s * 160 : (s + 1) * 160]) * keep).astype(BF)
        return carry

    lax.fori_loop(0, 8, expand, 0)
    for s in range(2):
        out[s] = dot(p5[...], dc[s]).astype(BF)

    pair.wait_send()
    flags.wait_send()
    swap.wait_send()
    for i in range(4):
        for copy in halo(i) + back(i):
            copy.wait_send()
    for copy in along_z() + second():
        copy.wait_send()

    def go(core):
        for copy in third(core) + relay(core) + [across(core, n) for n in range(4)]:
            copy.wait_send()

    on_core(go)


def shards(fields, valid_rows, fine_qkv, fine_out, merge_weight, coarse_qkv, coarse_out, expand_weight):
    early, late = tables()
    xp = jnp.pad(fields, ((0, 0), (0, 0), (0, 0), (0, 4), (0, 0))).reshape(2, 4, 192, 512)
    valid = jnp.pad(valid_rows, (0, 4)).astype(BF)
    fl = jnp.concatenate(
        [jnp.broadcast_to(valid[:, None], (16, 128)), jnp.broadcast_to(jnp.pad(valid, (0, 112))[None], (16, 128))], axis=0
    )
    block = jnp.concatenate([coarse_qkv, coarse_out[None]], axis=0)
    is_first = lax.axis_index("lon") % 2 == 0
    cw = jnp.where(
        is_first, jnp.pad(block, ((0, 0), (0, 0), (0, 64))), jnp.pad(block, ((0, 0), (0, 0), (64, 0)))
    )
    operands = [xp, fl, cw] + early + late + [fine_qkv, fine_out, merge_weight, expand_weight]
    vmem = pl.BlockSpec(memory_space=pltpu.VMEM)
    anywhere = pl.BlockSpec(memory_space=pl.ANY)
    dma = pltpu.SemaphoreType.DMA
    scratch = [pltpu.VMEM(a.shape, BF) for a in late]
    scratch += [pltpu.VMEM(a.shape, BF) for a in (fine_qkv, fine_out, merge_weight, expand_weight)]
    scratch += [pltpu.VMEM((4, 320, 512), BF)] * 4
    scratch += [pltpu.VMEM((32, 128), BF), pltpu.VMEM((4, 64, 128), BF)]
    scratch += [pltpu.VMEM((2, 4, 4, 8, 2, 2, 32, 128), BF)]
    scratch += [pltpu.VMEM((288, 512), F32)] + [pltpu.VMEM((288, 512), BF)] * 4
    scratch += [pltpu.VMEM((288, 128), F32), pltpu.VMEM((2, 2, 144, 144), F32)]
    scratch += [pltpu.VMEM((PADC, 2 * PADC), F32), pltpu.VMEM((2, 2 * PADC, 128), F32)]
    scratch += [pltpu.VMEM((2, 640, 512), BF), pltpu.VMEM((4, 320, 512), BF)]
    scratch += [pltpu.VMEM((320, 1024), BF), pltpu.VMEM((2, 320, 1024), BF)]
    scratch += [pltpu.VMEM((320, 1024), BF), pltpu.VMEM((2, 640, 1024), BF)]
    scratch += [pltpu.VMEM((320, 1024), BF)] * 2 + [pltpu.VMEM((2, 640, 512), BF)]
    for shape in ((4, 3), (4, 3), (1,), (1,), (7,), (3,), (2,), (2,), (4,), (1,)):
        scratch += [dma(shape), dma(shape)]
    scratch += [dma((8,))]
    result = pl.pallas_call(
        kernel,
        out_shape=jax.ShapeDtypeStruct((2, 768, 512), BF),
        in_specs=[vmem] * (3 + len(early)) + [anywhere] * 8,
        out_specs=vmem,
        scratch_shapes=scratch,
        compiler_params=pltpu.CompilerParams(collective_id=0, has_side_effects=True, vmem_limit_bytes=60 * 2**20),
    )(*operands)
    return result.reshape(2, 4, 12, 16, 512)[:, :, :, :12]


def solution(mesh):
    return jax.shard_map(
        shards,
        mesh=mesh,
        in_specs=(
            P(None, None, "lat", "lon", None),
            P("lat"),
            P(),
            P(),
            P(),
            P(None, "lat", "lon"),
            P("lat", "lon"),
            P(),
        ),
        out_specs=P(None, None, "lat", "lon", None),
        check_vma=False,
    )
```

time: 324 us -> 99.2 us (0.31)
  the two profiles are of different devices: /device:TPU:2 before, /device:TPU:1 now
where the time goes in v1:
time: 99.2 us; the launch traced here: 97.7 us
  Pallas kernels  88.3 us (89%)
  local copies, waits for them, and re-layouts  6.53 us (7%)
  other arithmetic  2.88 us (3%)
    pallas_call x1, Pallas kernels, shards(): pl.pallas_call(kernel, out_shape=jax.ShapeDtypeStruct((2, 768, 512), BF),...  88.3 us
    unnamed x2, local copies, waits for them, and re-layouts  5.1 us

profile of v1, /device:TPU:1, one launch (start us, length us, event | category | flops | bytes accessed | tf_op | source)
XLA Modules:
  0.0 97.7 jit_solution(17833936396981971786)
XLA Ops:
  0.0 0.7 convert.4
  0.7 0.7 pad_maximum_fusion.1.fl
  1.4 0.8 pad_maximum_fusion
  2.2 0.7 pad_select_fusion.cw
  2.9 1.6 %copy.25 = bf16[2,4,12,12,512]{4,3,2,1,0:T(8,128)(2,1)S(1)} copy(bf16[2,4,12,12,512]{4,1,3,2,0:T(4,128)(2,1)} %param.21) | data formatting | bytes 2359296
  4.5 1.4 %pad.21.clone = bf16[2,4,12,16,512]{4,3,2,1,0:T(8,128)(2,1)} pad(bf16[2,4,12,12,512]{4,3,2,1,0:T(8,128)(2,1)S(1)} %copy.25, bf16[]{:T(256)} %constant.42.clone.1), padding=0_0x0_0x0_0x0_4x0_0 | pad | bytes 2752514 | tf_op jit(solution)/shard_map/jit(_pad)/pad | solution.py:438
  5.9 88.3 %shard_map.199 = bf16[2,768,512]{2,1,0:T(8,128)(2,1)} custom-call(bf16[2,4,192,512]{3,2,1,0:T(8,128)(2,1)} %bitcast.4, bf16[32,128]{1,0:T(8,128)(2,1)} %pad_maximum_fusion.1.fl, bf16[4,64,128]{2,1,0:T(8,128)(2,1)} %pad_select_fusion.cw, bf16[2,320,192]{2,1,0:T(8,128)(2,1)} %constant.47.clone.p1, bf16[2,144,32]{2,1,0:T(8,128)(2,1)} %constant.48.clone.r1, ...), custom_call_target="tpu_custom_call" | custom-call | tf_op jit(solution)/shard_map/pallas_call | solution.py:467
  94.2 3.5 %copy.24 = bf16[2,4,12,12,512]{4,1,3,2,0:T(4,128)(2,1)} copy(bf16[2,4,12,12,512]{4,3,2,1,0:T(8,128)(2,1)} %bitcast.5) | data formatting | bytes 2359296
  (4 shorter events, 0.0 us)

commit v2 on v1

v2 whole, which is shorter than its diff:
```python
import functools
import math

import jax
import jax.numpy as jnp
import numpy as np
from jax import lax
from jax.experimental import pallas as pl
from jax.experimental.pallas import tpu as pltpu
from jax.sharding import PartitionSpec as P

BF = jnp.bfloat16
F32 = jnp.float32
MESH = pl.DeviceIdType.MESH
EPSILON = 1e-05
NEG = -1e30
QSCALE = 32 ** (-0.5) * math.log2(math.e)

SEG = dict(A0=(0, 144), B0=(144, 288), A1=(288, 368), B1=(368, 448), C=(448, 528), D=(528, 608))
TOKENS = 608
REMOTE = ("B0", "B1", "C", "D")
UNIT = ((0, 288), (288, 608))
LEVELS = ((1, 2), (3, 0))
PADC = 80


def segment_row(level_index, r, c):
    east = c >= 6
    if 3 <= r < 9:
        name, rows, row = "A0" if east else "B0", 6, r - 3
    elif r >= 9:
        name, rows, row = "A1" if east else "B1", 3, r - 9
    else:
        name, rows, row = "C" if east else "D", 3, r
    return SEG[name][0] + (level_index * rows + row) * 6 + c % 6


def window_row(level_index, r, c):
    row = r - 3 if 3 <= r < 9 else (r - 9 if r >= 9 else r + 3)
    column = c - 6 if c >= 6 else c + 6
    return level_index * 72 + row * 12 + column


def coarse_row(level, row, column):
    return (level // 2) * PADC + (level % 2) * 36 + row * 6 + column


def tables():
    p1 = np.zeros((TOKENS, 576), np.float32)
    p2 = np.zeros((288, TOKENS), np.float32)
    p4 = np.zeros((4 * 2 * PADC, TOKENS), np.float32)
    p5 = np.zeros((576, 4 * 2 * PADC), np.float32)
    for r in range(12):
        for c in range(12):
            plane = (r % 2) + 2 * (c % 2)
            for index in range(4):
                level = LEVELS[index // 2][index % 2]
                seg = segment_row(index, r, c)
                place = (r * 12 + c) * 4 + level
                low = plane * 2 * PADC + coarse_row(level, r // 2, c // 2)
                p1[seg, place] = 1
                p2[window_row(index, r, c), seg] = 1
                p4[low, seg] = 1
                p5[place, low] = 1
    rows = np.zeros((2, 144, 32), np.float32)
    differ = np.zeros((144, 144), np.float32)
    level = np.zeros((144, 144), np.float32)
    for t in range(144):
        r6 = (t % 72) // 12
        rows[0, t, 3 + r6] = 1
        rows[1, t, 9 + r6 if r6 < 3 else 16 + r6 - 3] = 1
        for u in range(144):
            differ[t, u] = (r6 < 3) != ((u % 72) // 12 < 3)
            level[t, u] = (t // 72) != (u // 72)
    rows_t = np.zeros((2, 256, 144), np.float32)
    rows_t[:, 0:12] = rows.transpose(0, 2, 1)[:, 0:12]
    rows_t[:, 128:131] = rows.transpose(0, 2, 1)[:, 16:19]
    coarse = np.zeros((PADC, 16), np.float32)
    keep = np.zeros((2, 2 * PADC, 16), np.float32)
    for t in range(72):
        row = (t % 36) // 6
        coarse[t, 2 * row] = 1
        for group in range(2):
            for parity in range(2):
                keep[parity, group * PADC + t, 2 * row + parity] = 1
    coarse_t = np.zeros((128, 2 * PADC), np.float32)
    coarse_t[0:16, :PADC] = coarse.T
    coarse_t[0:16, PADC:] = coarse.T
    pads = np.zeros((8, 2 * PADC), np.float32)
    pads[:, np.arange(2 * PADC) % PADC >= 72] = 1
    ways = [p2[:, low:high] for low, high in UNIT]
    half = [p1, rows, rows_t, coarse, coarse_t, keep] + ways + [w.T.copy() for w in ways] + [p4, p5]
    return [jnp.asarray(a, BF) for a in half] + [jnp.asarray(a, F32) for a in (level, differ, pads)]


def dot(a, b):
    return jnp.dot(a, b, preferred_element_type=F32)


def dot_nt(a, b):
    return lax.dot_general(a, b, (((1,), (1,)), ((), ())), preferred_element_type=F32)


def normalised(x, width):
    mean = jnp.sum(x, axis=-1, keepdims=True) * (1.0 / width)
    centre = x - mean
    spread = jnp.sum(centre * centre, axis=-1, keepdims=True) * (1.0 / width)
    return centre * lax.rsqrt(spread + EPSILON)


def head_masks():
    head = lax.broadcasted_iota(jnp.int32, (16, 128), 1) // 32
    return [jnp.where(head == h, 1.0, 0.0).astype(BF)[0:1] for h in range(4)]


def weighed(expo, v4, mask):
    return dot(expo, jnp.concatenate([v4 * mask, jnp.broadcast_to(mask, v4.shape)], axis=1))


def attention(q4, k4, v4, bias, together):
    masks = head_masks()
    count = q4.shape[0]
    if together:
        scores = dot_nt(jnp.concatenate([q4 * m for m in masks], axis=0), k4)
    total = 0.0
    for h, mask in enumerate(masks):
        mine = (scores[h * count : (h + 1) * count] if together else dot_nt(q4 * mask, k4)) + bias
        expo = jnp.exp2(mine - jnp.max(mine, axis=-1, keepdims=True)).astype(BF)
        total = total + weighed(expo, v4, mask)
    return (total[:, :128] / total[:, 128:]).astype(BF)


def kernel(
    xp, vr, cqkv, cout, *rest
):
    tabs_h, (wqkv_h, wo_h, wm_h, we_h), out, rest = rest[:15], rest[15:19], rest[19], rest[20:]
    tabs, (wqkv, wo, wm, we), rest = rest[:15], rest[15:19], rest[19:]
    p1, r1, rt, rc, rct, rk, p2a, p2b, p3a, p3b, p4, p5, lm, dm, pads = tabs
    snd, xb, ret, zb, fl, fln, cw, pb, wg, xw, q, k, v, at, kcol, bias, cbias, krow, *rest = rest
    skp, nbm, mg, n2, q2, kv2, a2, co, dc, *rest = rest
    hs, hr, rs, rr, fs, fr, ps, pr, zs, zr, s2s, s2r, s3s, s3r, ds_, dr, ns, nr, ws = rest
    lat = lax.axis_index("lat")
    lon = lax.axis_index("lon")
    z, y_hi = lat // 2, lat % 2
    y_lo, x, c = lon // 8, (lon // 2) % 4, lon % 2
    y = y_hi * 2 + y_lo

    def device(z_, y_, x_, c_):
        return (z_ * 2 + y_ // 2, (y_ % 2) * 8 + x_ * 2 + c_)

    north, south = (lat + 15) % 16, (lat + 1) % 16
    west, east = (lon + 15) % 16, (lon + 1) % 16
    partner = device(z, y, x, 1 - c)

    barrier = pltpu.get_barrier_semaphore()
    greeted = [partner, (lat, west), (lat, east), (north, lon), (south, lon), (north, west), (south, east)]
    greeted += [device((z + d) % 8, y, x, c) for d in range(1, 8)]
    greeted += [device(z, (y + d) % 4, x, c) for d in range(1, 4)]
    greeted += [device(z, y, (x + d) % 4, c) for d in range(1, 4)]
    for target in greeted:
        pl.semaphore_signal(barrier, inc=1, device_id=target, device_id_type=MESH)

    order = list(range(15)) + [15, 16, 17, 18]
    pairs_ = list(zip(list(tabs_h) + [wqkv_h, wo_h, wm_h, we_h], list(tabs) + [wqkv, wo, wm, we]))
    loads = [pltpu.make_async_copy(*pairs_[n], ws.at[n]) for n in order]
    for n in (0, 1, 2, 3, 4, 5, 12, 13, 14, 6, 7, 15, 16, 8, 9, 10, 17, 18, 11):
        loads[n].start()

    def remote(src, dst, send, recv, target):
        return pltpu.make_async_remote_copy(
            src_ref=src, dst_ref=dst, send_sem=send, recv_sem=recv, device_id=target, device_id_type=MESH
        )

    def segments(source, target, send, recv, s, across_lon, across_lat, names):
        places = (("B0", (lat, across_lon)), ("B1", (lat, across_lon)), ("C", (across_lat, lon)), ("D", (across_lat, across_lon)))
        return [
            remote(source.at[s, slice(*SEG[name])], target.at[s, slice(*SEG[name])], send.at[s, n], recv.at[s, n], to)
            for n, (name, to) in enumerate(places)
            if name in names
        ]

    def halo(s, names=REMOTE):
        return segments(snd, xb, hs, hr, s, west, north, names)

    def back(s, names=REMOTE):
        return segments(ret, zb, rs, rr, s, east, south, names)

    flags = remote(fl, fln, fs.at[0], fr.at[0], (north, lon))
    pair = remote(cw, pb, ps.at[0], pr.at[0], partner)

    qkv_part, out_part = slice(0, 3), slice(3, 4)

    def along_z(n, m):
        block = wg.at[y_lo, x, m, z, y_hi, c]
        return [
            remote(block, block, zs.at[n, d - 1], zr.at[n, d - 1], device((z + d) % 8, y, x, c)) for d in range(1, 8)
        ]

    def second(n, m):
        block = wg.at[y_lo, x, m, :, y_hi, c]
        return [
            remote(block, block, s2s.at[n, d - 1], s2r.at[n, d - 1], device(z, (y + d * (1 - c)) % 4, (x + d * c) % 4, c))
            for d in range(1, 4)
        ]

    def chunk(core, step, m):
        if core == 0:
            return wg.at[:, (x + step) % 4, m, :, :, 0]
        other = (y + step) % 4
        return wg.at[other % 2, :, m, :, other // 2, 1]

    def ring(core, step):
        return device(z, y, (x + step) % 4, core) if core == 0 else device(z, (y + step) % 4, x, core)

    def third(core, m):
        block = chunk(core, 0, slice(m, m + 1))
        return [remote(block, block, s3s.at[m, d - 1], s3r.at[m, d - 1], ring(core, d)) for d in range(1, 4)]

    def across(core, m, d):
        block = chunk(core, (4 - d) % 4, slice(m, m + 1))
        return remote(block, block, ds_.at[m, d], dr.at[m, d], partner)

    def on_core(action):
        @pl.when(c == 0)
        def _():
            action(0)

        @pl.when(c == 1)
        def _():
            action(1)

    pl.semaphore_wait(barrier, len(greeted))
    place = lax.broadcasted_iota(jnp.int32, (64, 128), 1) == lax.broadcasted_iota(jnp.int32, (64, 128), 0) + 64 * c
    place = jnp.where(place, 1.0, 0.0).astype(BF)
    cw[0:3] = dot(cqkv[...].reshape(192, 64), place).astype(BF).reshape(3, 64, 128)
    cw[3] = dot(cout[...], place).astype(BF)
    pair.start()
    spread = jnp.where(
        lax.broadcasted_iota(jnp.int32, (12, 128), 1) == lax.broadcasted_iota(jnp.int32, (12, 128), 0), 1.0, 0.0
    )
    flat = dot(jnp.broadcast_to(vr[...].astype(F32), (16, 12)).astype(BF), spread.astype(BF))
    corner = lax.broadcasted_iota(jnp.int32, (16, 128), 1) == lax.broadcasted_iota(jnp.int32, (16, 128), 0)
    fl[16:32] = flat.astype(BF)
    fl[0:16] = dot(jnp.where(corner, flat, 0.0).astype(BF), jnp.ones((128, 128), BF)).astype(BF)
    flags.start()

    pair.wait_recv()
    block = cw[...] + pb[...]
    wg[y_lo, x, :, z, y_hi, c] = jnp.where(c == 0, block[:, :32], block[:, 32:])
    for copy in along_z(0, qkv_part):
        copy.start()

    loads[0].wait()
    for s in range(2):
        tokens = dot(p1[...], xp[s * 144 : (s + 1) * 144].reshape(576, 512)).astype(BF)
        snd[s] = tokens
        for name in ("A0", "A1"):
            xb[s, slice(*SEG[name])] = tokens[slice(*SEG[name])]
        for copy in halo(s):
            copy.start()

    def poll_z():
        for copy in along_z(0, qkv_part):
            copy.wait_recv()
        for copy in second(0, qkv_part) + along_z(1, out_part):
            copy.start()

    def poll_second():
        for copy in second(0, qkv_part) + along_z(1, out_part):
            copy.wait_recv()

        def go(core):
            for m in range(3):
                for copy in third(core, m):
                    copy.start()
            for m in range(3):
                across(core, m, 0).start()

        on_core(go)
        for copy in second(1, out_part):
            copy.start()

    def poll_third(m):
        def go(core):
            arrivals = third(core, m)
            for d in (1, 3, 2):
                arrivals[d - 1].wait_recv()
                across(core, m, d).start()

        on_core(go)

    def poll_out():
        for copy in second(1, out_part):
            copy.wait_recv()

        def go(core):
            for copy in third(core, 3) + [across(core, 3, 0)]:
                copy.start()

        on_core(go)

    def arrived(m):
        def go(core):
            for d in range(4):
                across(core, m, d).wait_recv()

        on_core(go)

    flags.wait_recv()
    for n in (1, 2, 3, 4, 5, 12, 13, 14):
        loads[n].wait()
    own, following = fl[...], fln[...]
    seam = jnp.where(lat == 15, NEG, 0.0)
    for w in range(2):
        down = dot(r1[w, :, 0:16], own[0:16]) + dot(r1[w, :, 16:32], following[0:16])
        flat = dot(own[16:32], rt[w, 0:128]) + dot(following[16:32], rt[w, 128:256])
        kcol[w * 144 : (w + 1) * 144] = down
        forbid = ((1.0 - flat[0:1]) * down[:, 0:1]) * NEG
        if w == 1:
            forbid = forbid + dm[...] * seam
        bias[0, w] = forbid
        bias[1, w] = forbid + lm[...] * NEG
    down = dot(rc[...], own[0:16])
    flat = dot(own[16:32], rct[...])
    cbias[...] = ((1.0 - flat[0:1]) * down[:, 0:1] + pads[0:1]) * NEG
    for parity in range(2):
        krow[parity] = dot(rk[parity], own[0:16])

    for n in (6, 7, 15, 16, 8, 9):
        loads[n].wait()

    def fine(s, w, after_qkv):
        for copy in halo(s, (("B0",), ("B1", "C", "D"))[w]):
            copy.wait_recv()
        low, high = UNIT[w]
        tokens = dot((p2a, p2b)[w][...], xb[s, low:high])
        xw[...] = tokens
        normed = normalised(tokens, 512).astype(BF)
        q[...] = (dot(normed, wqkv[:, 0:512]) * QSCALE).astype(BF)
        k[...] = dot(normed, wqkv[:, 512:1024]).astype(BF)
        v[...] = dot(normed, wqkv[:, 1024:1536]).astype(BF)
        after_qkv()
        for g in range(4):
            lanes = slice(g * 128, (g + 1) * 128)
            for group in range(2):
                rows = slice(group * 144, (group + 1) * 144)
                at[rows, lanes] = attention(q[rows, lanes], k[rows, lanes], v[rows, lanes], bias[group, w], False)
        keep = kcol[w * 144 : (w + 1) * 144, 0:1]
        skip = (xw[...] + dot(at[...], wo[...])).reshape(2, 144, 512) * keep[None]
        tokens = dot((p3a, p3b)[w][...], skip.reshape(288, 512).astype(BF)).astype(BF)
        ret[s, low:high] = tokens
        name = ("A0", "A1")[w]
        zb[s, slice(*SEG[name])] = tokens[slice(SEG[name][0] - low, SEG[name][1] - low)]
        for copy in back(s, (("B0",), ("B1", "C", "D"))[w]):
            copy.start()

    def nothing():
        return None

    fine(0, 0, poll_z)
    fine(0, 1, poll_second)
    fine(1, 1, nothing)
    fine(1, 0, nothing)
    for n in (10, 17, 18, 11):
        loads[n].wait()

    for s in range(2):
        for copy in back(s):
            copy.wait_recv()
        planes = dot(p4[...], zb[s])
        skp[s] = planes.astype(BF)
        planes = planes.reshape(4, 160, 512)
        mean = jnp.sum(jnp.sum(planes, axis=0), axis=-1, keepdims=True) * (1.0 / 2048)
        centre = planes - mean[None]
        spread = jnp.sum(jnp.sum(centre * centre, axis=0), axis=-1, keepdims=True) * (1.0 / 2048)
        nbm[:, s * 160 : (s + 1) * 160] = (centre * lax.rsqrt(spread + EPSILON)[None]).astype(BF)

    def merge(n, carry):
        lanes = pl.ds(pl.multiple_of(n * 256, 256), 256)
        total = dot(nbm[0], wm[0:512, lanes])
        for p in range(1, 4):
            total = total + dot(nbm[p], wm[512 * p : 512 * (p + 1), lanes])
        mg[:, lanes] = total.astype(BF)
        return carry

    lax.fori_loop(0, 4, merge, 0)
    n2[0] = normalised(mg[...].astype(F32), 1024).astype(BF)
    swap = remote(n2.at[0], n2.at[1], ns.at[0], nr.at[0], partner)
    swap.start()

    poll_third(0)
    poll_third(1)
    arrived(0)

    def weights(matrix, n):
        low = (n % 2) * 2
        pieces = [wg[n // 2, low + j, matrix].reshape(1024, 128) for j in range(2)]
        return jnp.concatenate(pieces, axis=1)

    def queries(n, carry):
        lanes = pl.ds(pl.multiple_of(n * 256, 256), 256)
        q2[:, lanes] = (dot(n2[0], weights(0, n)) * QSCALE).astype(BF)
        return carry

    lax.fori_loop(0, 4, queries, 0)
    poll_third(2)
    poll_out()
    swap.wait_recv()

    def keys(matrix, block, carry):
        lanes = pl.ds(pl.multiple_of(block * 256, 256), 256)
        kv2[matrix, :, lanes] = dot(n2[...].reshape(640, 1024), weights(matrix + 1, block)).astype(BF)
        return carry

    for matrix in range(2):
        arrived(1 + matrix)
        lax.fori_loop(0, 4, functools.partial(keys, matrix), 0)

    def heads(half, carry):
        for g in range(4):
            lanes = pl.ds(pl.multiple_of(half * 512 + g * 128, 128), 128)
            for j in range(4):
                rows, far = slice(j * PADC, (j + 1) * PADC), slice(320 + j * PADC, 320 + (j + 1) * PADC)
                k4 = jnp.concatenate([kv2[0, rows, lanes], kv2[0, far, lanes]], axis=0)
                v4 = jnp.concatenate([kv2[1, rows, lanes], kv2[1, far, lanes]], axis=0)
                a2[rows, lanes] = attention(q2[rows, lanes], k4, v4, cbias[...], True)
        return carry

    lax.fori_loop(0, 2, heads, 0)
    poll_third(3)
    arrived(3)

    def project(n, carry):
        lanes = pl.ds(pl.multiple_of(n * 256, 256), 256)
        co[:, lanes] = (mg[:, lanes].astype(F32) + dot(a2[...], weights(3, n))).astype(BF)
        return carry

    lax.fori_loop(0, 4, project, 0)

    def expand(n, carry):
        plane, side = n // 2, n % 2
        grown = dot(co[...], we[:, pl.ds(pl.multiple_of(n * 256, 256), 256)])
        rows = pl.ds(pl.multiple_of(plane * 160, 160), 160)
        lanes = pl.ds(pl.multiple_of(side * 256, 256), 256)
        keep = krow[plane % 2][:, 0:1]
        for s in range(2):
            dc[s, rows, lanes] = ((skp[s, rows, lanes].astype(F32) + grown[s * 160 : (s + 1) * 160]) * keep).astype(BF)
        return carry

    lax.fori_loop(0, 8, expand, 0)
    for s in range(2):
        out[s * 144 : (s + 1) * 144] = dot(p5[...], dc[s]).astype(BF).reshape(144, 4, 512)

    pair.wait_send()
    flags.wait_send()
    swap.wait_send()
    for s in range(2):
        for copy in halo(s) + back(s):
            copy.wait_send()
    for n, m in enumerate((qkv_part, out_part)):
        for copy in along_z(n, m) + second(n, m):
            copy.wait_send()

    def go(core):
        for m in range(4):
            for copy in third(core, m) + [across(core, m, d) for d in range(4)]:
                copy.wait_send()

    on_core(go)


def shards(fields, valid_rows, fine_qkv, fine_out, merge_weight, coarse_qkv, coarse_out, expand_weight):
    tabs = tables()
    xp = fields.transpose(0, 2, 3, 1, 4).reshape(288, 4, 512)
    operands = [xp, valid_rows.reshape(1, 12), coarse_qkv, coarse_out] + tabs
    operands += [fine_qkv, fine_out, merge_weight, expand_weight]
    vmem = pl.BlockSpec(memory_space=pltpu.VMEM)
    anywhere = pl.BlockSpec(memory_space=pl.ANY)
    dma = pltpu.SemaphoreType.DMA
    scratch = [pltpu.VMEM(a.shape, a.dtype) for a in tabs]
    scratch += [pltpu.VMEM(a.shape, BF) for a in (fine_qkv, fine_out, merge_weight, expand_weight)]
    scratch += [pltpu.VMEM((2, TOKENS, 512), BF)] * 4
    scratch += [pltpu.VMEM((32, 128), BF)] * 2 + [pltpu.VMEM((4, 64, 128), BF)] * 2
    scratch += [pltpu.VMEM((2, 4, 4, 8, 2, 2, 32, 128), BF)]
    scratch += [pltpu.VMEM((288, 512), F32)] + [pltpu.VMEM((288, 512), BF)] * 4
    scratch += [pltpu.VMEM((288, 128), F32), pltpu.VMEM((2, 2, 144, 144), F32)]
    scratch += [pltpu.VMEM((PADC, 2 * PADC), F32), pltpu.VMEM((2, 2 * PADC, 128), F32)]
    scratch += [pltpu.VMEM((2, 640, 512), BF), pltpu.VMEM((4, 320, 512), BF)]
    scratch += [pltpu.VMEM((320, 1024), BF), pltpu.VMEM((2, 320, 1024), BF)]
    scratch += [pltpu.VMEM((320, 1024), BF), pltpu.VMEM((2, 640, 1024), BF)]
    scratch += [pltpu.VMEM((320, 1024), BF)] * 2 + [pltpu.VMEM((2, 640, 512), BF)]
    for shape in ((2, 4), (2, 4), (1,), (1,), (2, 7), (2, 3), (4, 3), (4, 4), (1,)):
        scratch += [dma(shape), dma(shape)]
    scratch += [dma((19,))]
    result = pl.pallas_call(
        kernel,
        out_shape=jax.ShapeDtypeStruct((288, 4, 512), BF),
        in_specs=[vmem] * 4 + [anywhere] * 19,
        out_specs=vmem,
        scratch_shapes=scratch,
        compiler_params=pltpu.CompilerParams(collective_id=0, has_side_effects=True, vmem_limit_bytes=60 * 2**20),
    )(*operands)
    return result.reshape(2, 12, 12, 4, 512).transpose(0, 3, 1, 2, 4)


def solution(mesh):
    return jax.shard_map(
        shards,
        mesh=mesh,
        in_specs=(
            P(None, None, "lat", "lon", None),
            P("lat"),
            P(),
            P(),
            P(),
            P(None, "lat", "lon"),
            P("lat", "lon"),
            P(),
        ),
        out_specs=P(None, None, "lat", "lon", None),
        check_vma=False,
    )
```

time: 99.2 us -> 85.8 us (0.86)
  the two profiles are of different devices: /device:TPU:1 before, /device:TPU:25 now
where the time goes in v2:
time: 85.8 us; the launch traced here: 85.7 us
  Pallas kernels  82.9 us (97%)
  local copies, waits for them, and re-layouts  2.79 us (3%)
    pallas_call x1, Pallas kernels, shards(): pl.pallas_call(kernel, out_shape=jax.ShapeDtypeStruct((288, 4, 512), BF),...  82.9 us
    unnamed x1, local copies, waits for them, and re-layouts  2.79 us

profile of v2, /device:TPU:25, one launch (start us, length us, event | category | flops | bytes accessed | tf_op | source)
XLA Modules:
  0.0 85.7 jit_solution(16663522717352948513)
XLA Ops:
  0.0 82.9 %shard_map.217 = bf16[288,4,512]{2,1,0:T(4,128)(2,1)} custom-call(bf16[288,4,512]{2,1,0:T(4,128)(2,1)} %bitcast.8, s32[1,12]{1,0:T(1,128)} %bitcast.9, bf16[3,64,64]{2,1,0:T(8,128)(2,1)} %cqkv.1, bf16[64,64]{1,0:T(8,128)(2,1)} %cout.1, bf16[608,576]{1,0:T(8,128)(2,1)} %constant.30.clone.rest_0_, bf16[2,144,32]{2,1,0:T(8,128)(2,1)} %constant.31.clone.rest_1_, ...), custom_call_target="tpu_custom_call" | custom-call | tf_op jit(solution)/shard_map/pallas_call | solution.py:495
  82.9 2.8 %copy.25 = bf16[2,4,12,12,512]{4,1,3,2,0:T(4,128)(2,1)} copy(bf16[2,4,12,12,512]{4,1,3,2,0:T(4,128)(2,1)} %bitcast.7) | data formatting | bytes 2359296

commit v3 on v2

--- a/solution.py
+++ b/solution.py
@@ -188,19 +188,17 @@
     flags = remote(fl, fln, fs.at[0], fr.at[0], (north, lon))
     pair = remote(cw, pb, ps.at[0], pr.at[0], partner)
 
-    qkv_part, out_part = slice(0, 3), slice(3, 4)
-
-    def along_z(n, m):
-        block = wg.at[y_lo, x, m, z, y_hi, c]
+    def first():
+        block = wg.at[y_lo, x, :, z, y_hi, c]
         return [
-            remote(block, block, zs.at[n, d - 1], zr.at[n, d - 1], device((z + d) % 8, y, x, c)) for d in range(1, 8)
+            remote(block, block, s2s.at[d - 1], s2r.at[d - 1], device(z, (y + d * (1 - c)) % 4, (x + d * c) % 4, c))
+            for d in range(1, 4)
         ]
 
-    def second(n, m):
-        block = wg.at[y_lo, x, m, :, y_hi, c]
+    def along_z(core, m):
+        block = wg.at[:, x, m, z, :, 0] if core == 0 else wg.at[y_lo, :, m, z, y_hi, 1]
         return [
-            remote(block, block, s2s.at[n, d - 1], s2r.at[n, d - 1], device(z, (y + d * (1 - c)) % 4, (x + d * c) % 4, c))
-            for d in range(1, 4)
+            remote(block, block, zs.at[m, d - 1], zr.at[m, d - 1], device((z + d) % 8, y, x, core)) for d in range(1, 8)
         ]
 
     def chunk(core, step, m):
@@ -247,7 +245,7 @@
     pair.wait_recv()
     block = cw[...] + pb[...]
     wg[y_lo, x, :, z, y_hi, c] = jnp.where(c == 0, block[:, :32], block[:, 32:])
-    for copy in along_z(0, qkv_part):
+    for copy in first():
         copy.start()
 
     loads[0].wait()
@@ -259,26 +257,26 @@
         for copy in halo(s):
             copy.start()
 
-    def poll_z():
-        for copy in along_z(0, qkv_part):
+    def poll_first():
+        for copy in first():
             copy.wait_recv()
-        for copy in second(0, qkv_part) + along_z(1, out_part):
-            copy.start()
-
-    def poll_second():
-        for copy in second(0, qkv_part) + along_z(1, out_part):
-            copy.wait_recv()
 
         def go(core):
-            for m in range(3):
-                for copy in third(core, m):
+            for m in range(2):
+                for copy in along_z(core, m):
                     copy.start()
-            for m in range(3):
-                across(core, m, 0).start()
 
         on_core(go)
-        for copy in second(1, out_part):
-            copy.start()
+
+    def poll_z(m):
+        def go(core):
+            for copy in along_z(core, m):
+                copy.wait_recv()
+            later = along_z(core, m + 2) if m + 2 < 4 else []
+            for copy in third(core, m) + [across(core, m, 0)] + later:
+                copy.start()
+
+        on_core(go)
 
     def poll_third(m):
         def go(core):
@@ -289,22 +287,14 @@
 
         on_core(go)
 
-    def poll_out():
-        for copy in second(1, out_part):
-            copy.wait_recv()
-
-        def go(core):
-            for copy in third(core, 3) + [across(core, 3, 0)]:
-                copy.start()
-
-        on_core(go)
-
     def arrived(m):
         def go(core):
             for d in range(4):
                 across(core, m, d).wait_recv()
 
         on_core(go)
+
+    poll_first()
 
     flags.wait_recv()
     for n in (1, 2, 3, 4, 5, 12, 13, 14):
@@ -357,10 +347,13 @@
     def nothing():
         return None
 
-    fine(0, 0, poll_z)
-    fine(0, 1, poll_second)
+    fine(0, 0, nothing)
+    fine(0, 1, nothing)
     fine(1, 1, nothing)
+    poll_z(0)
     fine(1, 0, nothing)
+    poll_z(1)
+    poll_z(2)
     for n in (10, 17, 18, 11):
         loads[n].wait()
 
@@ -404,7 +397,7 @@
 
     lax.fori_loop(0, 4, queries, 0)
     poll_third(2)
-    poll_out()
+    poll_z(3)
     swap.wait_recv()
 
     def keys(matrix, block, carry):
@@ -457,13 +450,12 @@
     for s in range(2):
         for copy in halo(s) + back(s):
             copy.wait_send()
-    for n, m in enumerate((qkv_part, out_part)):
-        for copy in along_z(n, m) + second(n, m):
-            copy.wait_send()
+    for copy in first():
+        copy.wait_send()
 
     def go(core):
         for m in range(4):
-            for copy in third(core, m) + [across(core, m, d) for d in range(4)]:
+            for copy in along_z(core, m) + third(core, m) + [across(core, m, d) for d in range(4)]:
                 copy.wait_send()
 
     on_core(go)
@@ -489,7 +481,7 @@
     scratch += [pltpu.VMEM((320, 1024), BF), pltpu.VMEM((2, 320, 1024), BF)]
     scratch += [pltpu.VMEM((320, 1024), BF), pltpu.VMEM((2, 640, 1024), BF)]
     scratch += [pltpu.VMEM((320, 1024), BF)] * 2 + [pltpu.VMEM((2, 640, 512), BF)]
-    for shape in ((2, 4), (2, 4), (1,), (1,), (2, 7), (2, 3), (4, 3), (4, 4), (1,)):
+    for shape in ((2, 4), (2, 4), (1,), (1,), (4, 7), (3,), (4, 3), (4, 4), (1,)):
         scratch += [dma(shape), dma(shape)]
     scratch += [dma((19,))]
     result = pl.pallas_call(

time: 85.8 us -> 76.9 us (0.90)
  the two profiles are of different devices: /device:TPU:25 before, /device:TPU:1 now
where the time goes in v3:
time: 76.9 us; the launch traced here: 76.7 us
  Pallas kernels  73.9 us (96%)
  local copies, waits for them, and re-layouts  2.79 us (4%)
    pallas_call x1, Pallas kernels, shards(): pl.pallas_call(kernel, out_shape=jax.ShapeDtypeStruct((288, 4, 512), BF),...  73.9 us
    unnamed x1, local copies, waits for them, and re-layouts  2.79 us

profile of v3, /device:TPU:1, one launch (start us, length us, event | category | flops | bytes accessed | tf_op | source)
XLA Modules:
  0.0 76.7 jit_solution(10940582292627933435)
XLA Ops:
  0.0 73.9 %shard_map.217 = bf16[288,4,512]{2,1,0:T(4,128)(2,1)} custom-call(bf16[288,4,512]{2,1,0:T(4,128)(2,1)} %bitcast.8, s32[1,12]{1,0:T(1,128)} %bitcast.9, bf16[3,64,64]{2,1,0:T(8,128)(2,1)} %cqkv.1, bf16[64,64]{1,0:T(8,128)(2,1)} %cout.1, bf16[608,576]{1,0:T(8,128)(2,1)} %constant.30.clone.rest_0_, bf16[2,144,32]{2,1,0:T(8,128)(2,1)} %constant.31.clone.rest_1_, ...), custom_call_target="tpu_custom_call" | custom-call | tf_op jit(solution)/shard_map/pallas_call | solution.py:487
  73.9 2.8 %copy.25 = bf16[2,4,12,12,512]{4,1,3,2,0:T(4,128)(2,1)} copy(bf16[2,4,12,12,512]{4,1,3,2,0:T(4,128)(2,1)} %bitcast.7) | data formatting | bytes 2359296

commit v4 on v3

--- a/solution.py
+++ b/solution.py
@@ -368,6 +368,8 @@
         spread = jnp.sum(jnp.sum(centre * centre, axis=0), axis=-1, keepdims=True) * (1.0 / 2048)
         nbm[:, s * 160 : (s + 1) * 160] = (centre * lax.rsqrt(spread + EPSILON)[None]).astype(BF)
 
+    poll_third(0)
+
     def merge(n, carry):
         lanes = pl.ds(pl.multiple_of(n * 256, 256), 256)
         total = dot(nbm[0], wm[0:512, lanes])
@@ -381,8 +383,9 @@
     swap = remote(n2.at[0], n2.at[1], ns.at[0], nr.at[0], partner)
     swap.start()
 
-    poll_third(0)
     poll_third(1)
+    poll_third(2)
+    poll_z(3)
     arrived(0)
 
     def weights(matrix, n):
@@ -396,8 +399,6 @@
         return carry
 
     lax.fori_loop(0, 4, queries, 0)
-    poll_third(2)
-    poll_z(3)
     swap.wait_recv()
 
     def keys(matrix, block, carry):

time: 76.9 us -> 77.7 us (1.010)
  Pallas kernels: 73.9 us -> 74.8 us
    pallas_call x1, Pallas kernels: 73.9 us -> 74.8 us  [shards(): pl.pallas_call(kernel, out_shape=jax.ShapeDtypeStruct((288, 4, 512), BF),...]
where the time goes in v4:
time: 77.7 us; the launch traced here: 77.6 us
  Pallas kernels  74.8 us (96%)
  local copies, waits for them, and re-layouts  2.79 us (4%)
    pallas_call x1, Pallas kernels, shards(): pl.pallas_call(kernel, out_shape=jax.ShapeDtypeStruct((288, 4, 512), BF),...  74.8 us
    unnamed x1, local copies, waits for them, and re-layouts  2.79 us

profile of v4, /device:TPU:1, one launch (start us, length us, event | category | flops | bytes accessed | tf_op | source)
XLA Modules:
  0.0 77.6 jit_solution(11708918793783701887)
XLA Ops:
  0.0 74.8 %shard_map.217 = bf16[288,4,512]{2,1,0:T(4,128)(2,1)} custom-call(bf16[288,4,512]{2,1,0:T(4,128)(2,1)} %bitcast.8, s32[1,12]{1,0:T(1,128)} %bitcast.9, bf16[3,64,64]{2,1,0:T(8,128)(2,1)} %cqkv.1, bf16[64,64]{1,0:T(8,128)(2,1)} %cout.1, bf16[608,576]{1,0:T(8,128)(2,1)} %constant.30.clone.rest_0_, bf16[2,144,32]{2,1,0:T(8,128)(2,1)} %constant.31.clone.rest_1_, ...), custom_call_target="tpu_custom_call" | custom-call | tf_op jit(solution)/shard_map/pallas_call | solution.py:488
  74.8 2.8 %copy.25 = bf16[2,4,12,12,512]{4,1,3,2,0:T(4,128)(2,1)} copy(bf16[2,4,12,12,512]{4,1,3,2,0:T(4,128)(2,1)} %bitcast.7) | data formatting | bytes 2359296

commit v5 on v3

--- a/solution.py
+++ b/solution.py
@@ -376,7 +376,7 @@
         mg[:, lanes] = total.astype(BF)
         return carry
 
-    lax.fori_loop(0, 4, merge, 0)
+    lax.fori_loop(0, 4, merge, 0, unroll=2)
     n2[0] = normalised(mg[...].astype(F32), 1024).astype(BF)
     swap = remote(n2.at[0], n2.at[1], ns.at[0], nr.at[0], partner)
     swap.start()
@@ -395,7 +395,7 @@
         q2[:, lanes] = (dot(n2[0], weights(0, n)) * QSCALE).astype(BF)
         return carry
 
-    lax.fori_loop(0, 4, queries, 0)
+    lax.fori_loop(0, 4, queries, 0, unroll=2)
     poll_third(2)
     poll_z(3)
     swap.wait_recv()
@@ -407,7 +407,7 @@
 
     for matrix in range(2):
         arrived(1 + matrix)
-        lax.fori_loop(0, 4, functools.partial(keys, matrix), 0)
+        lax.fori_loop(0, 4, functools.partial(keys, matrix), 0, unroll=2)
 
     def heads(half, carry):
         for g in range(4):
@@ -428,7 +428,7 @@
         co[:, lanes] = (mg[:, lanes].astype(F32) + dot(a2[...], weights(3, n))).astype(BF)
         return carry
 
-    lax.fori_loop(0, 4, project, 0)
+    lax.fori_loop(0, 4, project, 0, unroll=4)
 
     def expand(n, carry):
         plane, side = n // 2, n % 2
@@ -440,7 +440,7 @@
             dc[s, rows, lanes] = ((skp[s, rows, lanes].astype(F32) + grown[s * 160 : (s + 1) * 160]) * keep).astype(BF)
         return carry
 
-    lax.fori_loop(0, 8, expand, 0)
+    lax.fori_loop(0, 8, expand, 0, unroll=4)
     for s in range(2):
         out[s * 144 : (s + 1) * 144] = dot(p5[...], dc[s]).astype(BF).reshape(144, 4, 512)
 

time: 76.9 us -> 75.3 us (0.979)
  Pallas kernels: 73.9 us -> 72.4 us
    pallas_call x1, Pallas kernels: 73.9 us -> 72.4 us  [shards(): pl.pallas_call(kernel, out_shape=jax.ShapeDtypeStruct((288, 4, 512), BF),...]
where the time goes in v5:
time: 75.3 us; the launch traced here: 75.2 us
  Pallas kernels  72.4 us (96%)
  local copies, waits for them, and re-layouts  2.79 us (4%)
    pallas_call x1, Pallas kernels, shards(): pl.pallas_call(kernel, out_shape=jax.ShapeDtypeStruct((288, 4, 512), BF),...  72.4 us
    unnamed x1, local copies, waits for them, and re-layouts  2.79 us

profile of v5, /device:TPU:1, one launch (start us, length us, event | category | flops | bytes accessed | tf_op | source)
XLA Modules:
  0.0 75.2 jit_solution(6973561037810614742)
XLA Ops:
  0.0 72.4 %shard_map.217 = bf16[288,4,512]{2,1,0:T(4,128)(2,1)} custom-call(bf16[288,4,512]{2,1,0:T(4,128)(2,1)} %bitcast.8, s32[1,12]{1,0:T(1,128)} %bitcast.9, bf16[3,64,64]{2,1,0:T(8,128)(2,1)} %cqkv.1, bf16[64,64]{1,0:T(8,128)(2,1)} %cout.1, bf16[608,576]{1,0:T(8,128)(2,1)} %constant.30.clone.rest_0_, bf16[2,144,32]{2,1,0:T(8,128)(2,1)} %constant.31.clone.rest_1_, ...), custom_call_target="tpu_custom_call" | custom-call | tf_op jit(solution)/shard_map/pallas_call | solution.py:487
  72.4 2.8 %copy.25 = bf16[2,4,12,12,512]{4,1,3,2,0:T(4,128)(2,1)} copy(bf16[2,4,12,12,512]{4,1,3,2,0:T(4,128)(2,1)} %bitcast.7) | data formatting | bytes 2359296
